TPU v7x, 256 devices: a whole 4x4x8 slice. The times are simulated.
256 devices in a mesh: row: 16 (over y, z_hi), col: 16 (over z_lo, x, core).
Axes of the slice: x: 4, y: 4, z: 8 (z_hi: 4, z_lo: 2; z = z_hi * 2 + z_lo), core: 2. Of those that a mesh axis runs over, the one named last changes fastest.
Arguments:
- fock_matrix: bfloat16 [8192, 8192], P('row', 'col'), may hold values from -0.0625 to 0.0625
- intersection: bfloat16 [8192, 8192], P('row', 'col'), may hold values from -0.0625 to 0.0625
- density_panel: bfloat16 [1024, 8192], P('col', 'row'), may hold values from -6 to 6
- fock_mask: int32 [16, 16], P('row', 'col'), may hold values from 0 to 1, as said below
- intersection_mask: int32 [16, 16], P('row', 'col'), may hold values from 0 to 1, as said below
- density_mask: int32 [2, 16], P(None, 'row'), may hold values 0 or 1
Outputs:
- sigma_window: float32 [8192, 8192], P('row', 'col')
Inputs may be any that keep to these rules, and one draw needn't show every extreme that they name: `fock_mask`: each entry flags one 512 x 512 tile; the diagonal tiles are always present. `intersection_mask`: each entry flags one 512 x 512 tile; the diagonal tiles are always present.
All inputs are finite; a program needn't handle non-finite values. No bound on the sum of `density_mask` on one device may be relied on, other than what follows from the above.
Results may differ from a plain program's by a relative error of at most 0.0029.
Values may be sent and summed in bfloat16 or wider, within the bound.
A program may use at most 64 MiB of HBM per device.

v0:
```python
import jax
import jax.numpy as jnp
from jax import lax
from jax.sharding import PartitionSpec as P

B = 512
PW = 1024
PANELS = 1


def broadcast(value, axis, source):
    kept = jnp.where(lax.axis_index(axis) == source, value, 0).astype(value.dtype)
    return lax.psum(kept, axis)


def zero_masked(matrix, tile_mask):
    rows_t, cols_t = tile_mask.shape
    shaped = matrix.reshape(rows_t, matrix.shape[0] // rows_t, cols_t, matrix.shape[1] // cols_t)
    factor_keep = tile_mask.astype(matrix.dtype)[:, None, :, None]
    return (shaped * factor_keep).reshape(matrix.shape)


def make_partial(density, factor):
    return jnp.dot(density, factor, preferred_element_type=jnp.float32)


def per_device(
    fock_matrix, intersection, density_panel, fock_mask, intersection_mask, density_mask
):
    tile_order = B
    window_width = PANELS * PW
    window_tiles = window_width // tile_order
    tile_cols = fock_matrix.shape[1] // tile_order
    fock_tiles = zero_masked(fock_matrix, fock_mask)
    intersection_tiles = zero_masked(intersection, intersection_mask)
    gathered = lax.all_gather(density_panel, "col", axis=0, tiled=True)
    density_tiles = zero_masked(gathered, density_mask)
    right_half = lax.psum_scatter(
        make_partial(density_tiles, intersection_tiles), "row", scatter_dimension=0, tiled=True
    ).astype(jnp.bfloat16)
    left_half = lax.psum_scatter(
        make_partial(density_tiles, fock_tiles), "row", scatter_dimension=0, tiled=True
    ).astype(jnp.bfloat16)
    sources = (window_tiles + tile_cols - 1) // tile_cols
    received = [
        (
            broadcast(fock_tiles, "col", source),
            broadcast(intersection_tiles, "col", source),
            broadcast(fock_mask, "col", source),
            broadcast(intersection_mask, "col", source),
        )
        for source in range(sources)
    ]
    fock_strip = jnp.concatenate([item[0] for item in received], axis=1)
    intersection_strip = jnp.concatenate([item[1] for item in received], axis=1)
    right_piece = lax.all_gather(right_half, "row", axis=0, tiled=True)
    left_piece = lax.all_gather(left_half, "row", axis=0, tiled=True)
    first_term = jnp.dot(fock_strip, right_piece, preferred_element_type=jnp.float32)
    second_term = jnp.dot(intersection_strip, left_piece, preferred_element_type=jnp.float32)
    return first_term - second_term


def solution(mesh):
    placed = (
        P("row", "col"),
        P("row", "col"),
        P("col", "row"),
        P("row", "col"),
        P("row", "col"),
        P(None, "row"),
    )
    return jax.shard_map(
        per_device, mesh=mesh, in_specs=placed, out_specs=P("row", "col"), check_vma=False
    )
```

profile of v0, /device:TPU:32, one launch (start us, length us, event | category | flops | bytes accessed | tf_op | source)
XLA Modules:
  0.0 475.0 jit_solution(5411579563712437923)
XLA Ops:
  6.5 0.0 all-gather.4.cloned.1.call-start
  6.5 0.7 all-gather.4.cloned.1.call-update
  7.3 0.0 reduce-scatter.3.cloned.1.call-start
  8.0 0.7 convert_bitcast_fusion
  8.6 0.1 broadcast_bitcast_fusion
  8.7 37.8 %all-gather.4.cloned.1.call-done = bf16[1024,512]{1,0:T(8,128)(2,1)} async-done(((bf16[64,512]{1,0:T(8,128)(2,1)}), bf16[1024,512]{1,0:T(8,128)(2,1)}) %all-gather.4.cloned.1.call-update) | async-done | bytes 1048592 | tf_op jit(solution)/shard_map/all_gather | solution.py:36
  46.5 0.0 copy-start
  46.5 0.0 copy-start.1
  46.5 3.6 fusion.9
  50.1 0.0 reduce-scatter.3.cloned.1.call-update
  50.1 0.0 reduce-scatter.5.cloned.1.call-start
  50.8 0.0 copy-done
  50.8 0.0 copy-done.1
  50.8 2.1 fusion.7
  52.9 0.0 copy-start.2
  52.9 0.0 reduce-scatter.5.cloned.1.call-update
  52.9 0.0 all-reduce.3.cloned.1.call-start
  53.0 1.1 broadcast_select_fusion.3
  54.1 0.0 copy-done.2
  54.1 1.1 broadcast_select_fusion.2
  55.1 0.0 all-reduce.3.cloned.1.call-update
  55.1 0.0 all-gather.6.cloned.1.call-start
  55.2 82.9 %reduce-scatter.3.cloned.1.call-done = f32[64,512]{1,0:T(8,128)} async-done(((f32[1024,512]{1,0:T(8,128)}), f32[64,512]{1,0:T(8,128)}) %reduce-scatter.3.cloned.1.call-update) | async-done | bytes 131088 | tf_op jit(solution)/shard_map/reduce_scatter | solution.py:38
  138.1 1.5 convert_element_type.23
  139.6 0.0 all-gather.6.cloned.1.call-update
  139.7 0.0 all-gather.8.cloned.1.call-start
  139.7 88.3 %reduce-scatter.5.cloned.1.call-done = f32[64,512]{1,0:T(8,128)} async-done(((f32[1024,512]{1,0:T(8,128)}), f32[64,512]{1,0:T(8,128)}) %reduce-scatter.5.cloned.1.call-update) | async-done | bytes 131088 | tf_op jit(solution)/shard_map/reduce_scatter | solution.py:41
  228.0 1.5 convert_element_type.24
  229.5 0.0 all-gather.8.cloned.1.call-update
  229.5 126.9 %all-reduce.3.cloned.1.call-done = (bf16[512,512]{1,0:T(8,128)(2,1)}, bf16[512,512]{1,0:T(8,128)(2,1)}, bf16[512,512]{1,0:T(8,128)(2,1)}, bf16[512,512]{1,0:T(8,128)(2,1)}) async-done(((bf16[512,512]{1,0:T(8,128)(2,1)}, bf16[512,512]{1,0:T(8,128)(2,1)}, bf16[512,512]{1,0:T(8,128)(2,1)}, bf16[512,512]{1,0:T(8,128)(2,1)}), (bf16[512,512]{1,0:T(8,128)(2,1)}, bf16[512,512]{1,0:T(8,128)(2,1)}, ...) | async-done | bytes 2097168 | tf_op jit(solution)/shard_map/psum | solution.py:13
  356.5 0.0 copy-start.3
  356.5 0.0 copy-start.4
  356.5 55.7 %all-gather.6.cloned.1.call-done = bf16[1024,512]{1,0:T(8,128)(2,1)} async-done(((bf16[64,512]{1,0:T(8,128)(2,1)}), bf16[1024,512]{1,0:T(8,128)(2,1)}) %all-gather.6.cloned.1.call-update) | async-done | bytes 1048592 | tf_op jit(solution)/shard_map/all_gather | solution.py:56
  412.2 2.2 fusion
  414.4 50.9 %all-gather.8.cloned.1.call-done = bf16[1024,512]{1,0:T(8,128)(2,1)} async-done(((bf16[64,512]{1,0:T(8,128)(2,1)}), bf16[1024,512]{1,0:T(8,128)(2,1)}) %all-gather.8.cloned.1.call-update) | async-done | bytes 1048592 | tf_op jit(solution)/shard_map/all_gather | solution.py:57
  465.3 0.0 copy-done.3
  465.3 0.0 copy-done.4
  465.3 2.9 convolution_subtract_fusion
  (1 shorter events, 0.0 us)
Async XLA Ops:
  6.5 39.9 %all-gather.4.cloned.1.call-start = ((), (), s32[]{:S(2)}) async-start(), calls=%async_computation.2 | async-start | bytes 1114112 | tf_op jit(solution)/shard_map/all_gather | solution.py:36
  7.3 130.8 %reduce-scatter.3.cloned.1.call-start = ((), (), s32[]{:S(2)}) async-start(), calls=%async_computation.3 | async-start | bytes 2228224 | tf_op jit(solution)/shard_map/reduce_scatter | solution.py:38
  46.5 4.3 copy-start
  46.5 4.3 copy-start.1
  50.1 177.9 %reduce-scatter.5.cloned.1.call-start = ((), (), s32[]{:S(2)}) async-start(), calls=%async_computation.5 | async-start | bytes 2228224 | tf_op jit(solution)/shard_map/reduce_scatter | solution.py:41
  52.9 1.2 copy-start.2
  52.9 303.5 %all-reduce.3.cloned.1.call-start = ((), (), s32[]{:S(2)}) async-start(), calls=%async_computation.7 | async-start | bytes 4194304 | tf_op jit(solution)/shard_map/psum | solution.py:13
  55.1 357.0 %all-gather.6.cloned.1.call-start = ((), (), s32[]{:S(2)}) async-start(), calls=%async_computation.4 | async-start | bytes 1114112 | tf_op jit(solution)/shard_map/all_gather | solution.py:56
  139.7 325.6 %all-gather.8.cloned.1.call-start = ((), (), s32[]{:S(2)}) async-start(), calls=%async_computation.6 | async-start | bytes 1114112 | tf_op jit(solution)/shard_map/all_gather | solution.py:57
  356.5 108.8 %copy-start.3 = (bf16[512,512]{1,0:T(8,128)(2,1)S(1)}, bf16[512,512]{1,0:T(8,128)(2,1)}, u32[]{:S(2)}) copy-start(bf16[512,512]{1,0:T(8,128)(2,1)} %get-tuple-element.7) | copy-start | bytes 1572868
  356.5 108.8 %copy-start.4 = (bf16[512,512]{1,0:T(8,128)(2,1)S(1)}, bf16[512,512]{1,0:T(8,128)(2,1)}, u32[]{:S(2)}) copy-start(bf16[512,512]{1,0:T(8,128)(2,1)} %get-tuple-element.8) | copy-start | bytes 1572868
Sparse Core Ops, SparseCore 0:
  9.2 37.2 all-gather.3
  50.2 87.8 reduce-scatter.2
  142.1 85.8 reduce-scatter.4
  230.7 125.7 all-reduce.2
  358.7 53.3 all-gather.5
  414.5 50.7 all-gather.7
where the time goes:
time: 478 us; the launch traced here: 475 us
  waiting for transfers between devices  443 us (93%)
  between operations  14.8 us (3%)
  matrix products  10.8 us (2%)
  other arithmetic  5.87 us (1%)
    psum x1, waiting for transfers between devices, broadcast(): return lax.psum(kept, axis)  127 us
    reduce_scatter x1, waiting for transfers between devices, per_device(): lax.psum_scatter(make_partial(density_tiles, fock_tiles), 'row', scatter_...  88.3 us
    reduce_scatter x1, waiting for transfers between devices, per_device(): lax.psum_scatter(make_partial(density_tiles, intersection_tiles), 'row',...  82.9 us
    all_gather x1, waiting for transfers between devices, per_device(): right_piece = lax.all_gather(right_half, 'row', axis=0, tiled=True)  55.7 us
    all_gather x1, waiting for transfers between devices, per_device(): left_piece = lax.all_gather(left_half, 'row', axis=0, tiled=True)  50.9 us
    all_gather x1, waiting for transfers between devices, per_device(): gathered = lax.all_gather(density_panel, 'col', axis=0, tiled=True)  37.8 us
  transfers between devices with their start and end apart: 6, of which 6 were waited for; matrix products, arithmetic and copies ran while one was open for 2% of the time, Pallas kernels for 0%

commit v1 on v0

v1 whole, which is shorter than its diff:
```python
import jax
import jax.numpy as jnp
from jax import lax
from jax.experimental import pallas as pl
from jax.experimental.pallas import tpu as pltpu
from jax.sharding import PartitionSpec as P

MESH = pl.DeviceIdType.MESH
NC = 4
LN = 128
QR = 256
ZR = 64
SR = 16
TOP = 32000.0
TINY = 2.0**-100


def encode(value):
    amax = jnp.max(jnp.abs(value), axis=0, keepdims=True)
    t = jnp.ceil(jnp.log2(jnp.maximum(amax, TINY)))
    q = jnp.round(value * (jnp.exp2(-t) * TOP)).astype(jnp.int32).astype(jnp.int16)
    return q, t


def decode(q, t):
    return q.astype(jnp.int32).astype(jnp.float32) * (jnp.exp2(t) * (1.0 / TOP))


def kernel(
    f_ref, s_ref, d_ref, fm_ref, sm_ref, dm_ref, out_ref,
    w, dg, ys, yr, pf, zs, zr, yq, qg, strips, rn,
    d_ss, d_rs, c_ss, c_rs, t_ss, t_rs, t0_ss, t0_rs,
    ys_ss, ys_rs, zs_ss, zs_rs, za_ss, za_rs, ya_ss, ya_rs,
):
    row, col = lax.axis_index("row"), lax.axis_index("col")
    y, zh = row // 4, row % 4
    zl, x, core = col // 8, (col // 2) % 4, col % 2
    p = zl * 4 + x

    def group_peer(o):
        return (row, ((zl + o // 4) % 2) * 8 + ((x + o % 4) % 4) * 2 + core)

    def chip_of(o):
        return ((zl + o // 4) % 2) * 4 + (x + o % 4) % 4

    def y_peer(d):
        return (((y + d) % 4) * 4 + zh, col)

    def z_peer(d):
        return (y * 4 + (zh + d) % 4, col)

    core_peer = (row, zl * 8 + x * 2 + 1 - core)
    up, down = y_peer(1), y_peer(3)

    started = []

    def copy(src, dst, ss, rs, to):
        return pltpu.make_async_remote_copy(
            src_ref=src, dst_ref=dst, send_sem=ss, recv_sem=rs, device_id=to, device_id_type=MESH
        )

    def send(src, dst, ss, rs, to):
        c = copy(src, dst, ss, rs, to)
        c.start()
        started.append(c)
        return c

    barrier = pltpu.get_barrier_semaphore()
    partners = [group_peer(o) for o in range(1, 8)]
    partners += [core_peer, up, down] + [z_peer(d) for d in (1, 2, 3)]
    for to in partners:
        pl.semaphore_signal(barrier, inc=1, device_id=to, device_id_type=MESH)

    dmask = dm_ref[zl, 0].astype(jnp.float32)
    for d in range(4):
        rows = d_ref[(y + 2 + d) % 4]
        dg[d, p, core] = (rows.astype(jnp.float32) * dmask).astype(jnp.bfloat16)
    fmask = fm_ref[0, 0].astype(jnp.float32)
    smask = sm_ref[0, 0].astype(jnp.float32)
    pl.semaphore_wait(barrier, len(partners))

    d0 = [send(dg.at[0, p, core], dg.at[0, p, core], d_ss.at[0, o], d_rs.at[0, o], group_peer(o)) for o in range(1, 8)]
    d1 = [
        send(dg.at[pl.ds(1, 3), p, core], dg.at[pl.ds(1, 3), p, core], d_ss.at[1, o], d_rs.at[1, o], group_peer(o))
        for o in range(1, 8)
    ]

    s_all = (s_ref[...].astype(jnp.float32) * smask).astype(jnp.bfloat16)
    f_all = (f_ref[...].astype(jnp.float32) * fmask).astype(jnp.bfloat16)
    for n in range(NC):
        w[n, :, :LN] = s_all[:, n * LN : (n + 1) * LN]
        w[n, :, LN:] = f_all[:, n * LN : (n + 1) * LN]

    @pl.when(p == 0)
    def _():
        for i in range(4):
            strips[core, i] = f_all[i * 128 : (i + 1) * 128]
            strips[core, 4 + i] = s_all[i * 128 : (i + 1) * 128]
        for i in range(1, 8):
            copy(strips.at[core, i], strips.at[core, i], t0_ss.at[i], t0_rs, (row, 2 * i + core)).start()

    def strips_spread():
        @pl.when(p != 0)
        def _():
            copy(strips.at[core, p], strips.at[core, p], t0_ss.at[0], t0_rs, core_peer).wait_recv()

        for o in range(1, 8):
            @pl.when(chip_of(o) != 0)
            def _():
                copy(strips.at[core, p], strips.at[core, p], t_ss.at[o], t_rs.at[o], group_peer(o)).start()

    def strips_swap():
        @pl.when(p != 0)
        def _():
            for o in range(1, 8):
                copy(strips.at[core, p], strips.at[core, p], t_ss.at[o], t_rs.at[o], core_peer).wait_recv()

        return send(strips.at[core], strips.at[core], c_ss.at[2], c_rs.at[2], core_peer)

    def product(d, n):
        return jnp.dot(dg[d].reshape(QR, 512), w[n], preferred_element_type=jnp.float32)

    y_sent = {}

    def send_y(n, i, value):
        q, t = encode(value)
        ys[n, i, :QR] = q
        ys[n, i, QR:] = jnp.broadcast_to(t, (SR, LN)).astype(jnp.int32).astype(jnp.int16)
        y_sent[n, i] = send(ys.at[n, i], yr.at[n, i], ys_ss.at[n, i], ys_rs.at[n, i], down if i % 2 else up)

    def recv_y(n, i):
        y_sent[n, i].wait_recv()
        t = yr[n, i, QR:].astype(jnp.int32).astype(jnp.float32)[:1]
        return decode(yr[n, i, :QR], t)

    def a_opposite(n):
        v = product(0, n)
        send_y(n, 0, v[:, :LN])
        send_y(n, 1, v[:, LN:])

    def a_rest(n):
        v = product(3, n)
        send_y(n, 2, v[:, LN:])
        pf[n, 0] = v[:, :LN]
        v = product(1, n)
        send_y(n, 3, v[:, :LN])
        pf[n, 1] = v[:, LN:]

    def b(n):
        send_y(n, 4, pf[n, 0] + recv_y(n, 0))
        send_y(n, 5, pf[n, 1] + recv_y(n, 1))

    z_sent = {}

    def c(n):
        v = product(2, n)
        left = v[:, LN:] + recv_y(n, 2)
        right = v[:, :LN] + recv_y(n, 3)
        right = right + recv_y(n, 4)
        left = left + recv_y(n, 5)
        yq[n, 0] = right.reshape(4, ZR, LN)
        yq[n, 1] = left.reshape(4, ZR, LN)
        for d in (2, 1, 3):
            to = (zh + d) % 4
            q0, t0 = encode(yq[n, 0, to])
            q1, t1 = encode(yq[n, 1, to])
            zs[n, d, :ZR] = q0
            zs[n, d, ZR : 2 * ZR] = q1
            t = jnp.concatenate([jnp.broadcast_to(t0, (8, LN)), jnp.broadcast_to(t1, (8, LN))], axis=0)
            zs[n, d, 2 * ZR :] = t.astype(jnp.int32).astype(jnp.int16)
            z_sent[n, d] = send(zs.at[n, d], zr.at[n, d], zs_ss.at[n, d], zs_rs.at[n, d], z_peer(d))

    za_sent = {}

    def e(n):
        right, left = yq[n, 0, zh], yq[n, 1, zh]
        for d in (1, 3, 2):
            z_sent[n, d].wait_recv()
            t = zr[n, d, 2 * ZR :].astype(jnp.int32).astype(jnp.float32)
            right = right + decode(zr[n, d, :ZR], t[:1])
            left = left + decode(zr[n, d, ZR : 2 * ZR], t[8:9])
        qg[n, y, 0, zh] = right.astype(jnp.bfloat16)
        qg[n, y, 1, zh] = left.astype(jnp.bfloat16)
        mine = qg.at[n, y, :, zh]
        for d in (2, 1, 3):
            za_sent[n, d] = send(mine, mine, za_ss.at[n, d], za_rs.at[n, d], z_peer(d))

    ya_sent = {}

    def g(n):
        for d in (1, 3, 2):
            za_sent[n, d].wait_recv()
        mine = qg.at[n, y]
        ya_sent[n, 0] = send(mine, mine, ya_ss.at[n, 0], ya_rs.at[n, 0], up)
        ya_sent[n, 1] = send(mine, mine, ya_ss.at[n, 1], ya_rs.at[n, 1], down)

    def h(n):
        ya_sent[n, 0].wait_recv()
        part = qg.at[n, (y + 3) % 4, 0]
        ya_sent[n, 2] = send(part, part, ya_ss.at[n, 2], ya_rs.at[n, 2], up)
        ya_sent[n, 1].wait_recv()
        part = qg.at[n, (y + 1) % 4, 1]
        ya_sent[n, 3] = send(part, part, ya_ss.at[n, 3], ya_rs.at[n, 3], down)

    def k(n):
        ya_sent[n, 2].wait_recv()
        ya_sent[n, 3].wait_recv()
        for m in range(2):
            for q in range(4):
                for cc in range(16):
                    at = cc * 64 + q * 16
                    rn[m, at : at + 16] = qg[n, q, m, cc // 4, (cc % 4) * 16 : (cc % 4) * 16 + 16]
        total = None
        for m in range(2):
            for half in range(2):
                lhs = strips[half, 4 * m : 4 * m + 4].reshape(512, 512)
                part = jnp.dot(lhs, rn[m, half * 512 : (half + 1) * 512], preferred_element_type=jnp.float32)
                total = part if total is None else (total + part if m == 0 else total - part)
        out_ref[:, n * LN : (n + 1) * LN] = total

    for cp in d0:
        cp.wait_recv()
    swap0 = send(dg.at[0, :, core], dg.at[0, :, core], c_ss.at[0], c_rs.at[0], core_peer)
    swap0.wait_recv()
    a_opposite(0)
    a_opposite(1)
    for cp in d1:
        cp.wait_recv()
    tail = pl.ds(1, 3)
    swap1 = send(dg.at[tail, :, core], dg.at[tail, :, core], c_ss.at[1], c_rs.at[1], core_peer)
    swap1.wait_recv()
    a_rest(0)
    b(0)
    a_opposite(2)
    a_rest(1)
    b(1)
    strips_spread()
    c(0)
    a_opposite(3)
    a_rest(2)
    b(2)
    c(1)
    e(0)
    a_rest(3)
    b(3)
    c(2)
    e(1)
    g(0)
    c(3)
    e(2)
    g(1)
    h(0)
    swap2 = strips_swap()
    e(3)
    g(2)
    h(1)
    swap2.wait_recv()
    k(0)
    g(3)
    h(2)
    k(1)
    h(3)
    k(2)
    k(3)

    for cp in started:
        cp.wait_send()

    @pl.when(p == 0)
    def _():
        for i in range(1, 8):
            copy(strips.at[core, i], strips.at[core, i], t0_ss.at[i], t0_rs, core_peer).wait_send()

    for o in range(1, 8):
        @pl.when(chip_of(o) != 0)
        def _():
            copy(strips.at[core, p], strips.at[core, p], t_ss.at[o], t_rs.at[o], core_peer).wait_send()


def per_device(fock_matrix, intersection, density_panel, fock_mask, intersection_mask, density_mask):
    vmem = pl.BlockSpec(memory_space=pltpu.VMEM)
    smem = pl.BlockSpec(memory_space=pltpu.SMEM)
    dma = pltpu.SemaphoreType.DMA
    return pl.pallas_call(
        kernel,
        out_shape=jax.ShapeDtypeStruct((512, 512), jnp.float32),
        in_specs=[vmem, vmem, vmem, smem, smem, smem],
        out_specs=vmem,
        scratch_shapes=[
            pltpu.VMEM((NC, 512, 2 * LN), jnp.bfloat16),
            pltpu.VMEM((4, 8, 2, 16, 512), jnp.bfloat16),
            pltpu.VMEM((NC, 6, QR + SR, LN), jnp.int16),
            pltpu.VMEM((NC, 6, QR + SR, LN), jnp.int16),
            pltpu.VMEM((NC, 2, QR, LN), jnp.float32),
            pltpu.VMEM((NC, 4, 2 * ZR + SR, LN), jnp.int16),
            pltpu.VMEM((NC, 4, 2 * ZR + SR, LN), jnp.int16),
            pltpu.VMEM((NC, 2, 4, ZR, LN), jnp.float32),
            pltpu.VMEM((NC, 4, 2, 4, ZR, LN), jnp.bfloat16),
            pltpu.VMEM((2, 8, 128, 512), jnp.bfloat16),
            pltpu.VMEM((2, 1024, LN), jnp.bfloat16),
            dma((2, 8)), dma((2, 8)), dma((3,)), dma((3,)), dma((8,)), dma((8,)), dma((8,)), dma(()),
            dma((NC, 6)), dma((NC, 6)), dma((NC, 4)), dma((NC, 4)), dma((NC, 4)), dma((NC, 4)),
            dma((NC, 4)), dma((NC, 4)),
        ],
        compiler_params=pltpu.CompilerParams(
            collective_id=0, has_side_effects=True, vmem_limit_bytes=40 * 2**20
        ),
        cost_estimate=pl.CostEstimate(flops=2 * 2**30, bytes_accessed=3 * 2**20, transcendentals=0),
    )(
        fock_matrix,
        intersection,
        density_panel.reshape(4, 16, 512),
        fock_mask,
        intersection_mask,
        density_mask,
    )


def solution(mesh):
    placed = (
        P("row", "col"),
        P("row", "col"),
        P("col", "row"),
        P("row", "col"),
        P("row", "col"),
        P(None, "row"),
    )
    return jax.shard_map(
        per_device, mesh=mesh, in_specs=placed, out_specs=P("row", "col"), check_vma=False
    )
```

time: 478 us -> 83.2 us (0.17)
  waiting for transfers between devices: 443 us -> 0 us
  Pallas kernels: 0 us -> 75.6 us
  between operations: 14.8 us -> 1.32 us
  matrix products: 10.8 us -> 0 us
  other arithmetic: 5.87 us -> 0 us
    reduce_scatter x2 -> x0, waiting for transfers between devices: 171 us -> none  [the longest x1 88.3 us: per_device(): lax.psum_scatter(make_partial(density_tiles, fock_tiles), 'row', scatter_...]
    all_gather x3 -> x0, waiting for transfers between devices: 144 us -> none  [the longest x1 55.7 us: per_device(): right_piece = lax.all_gather(right_half, 'row', axis=0, tiled=True)]
    psum x1 -> x0, waiting for transfers between devices: 127 us -> none  [broadcast(): return lax.psum(kept, axis)]
    pallas_call x0 -> x1, Pallas kernels: none -> 75.6 us  [per_device(): pl.pallas_call(kernel, out_shape=jax.ShapeDtypeStruct((512, 512), jnp.flo...]
    dot_general x4 -> x0, matrix products: 10.8 us -> none  [the longest x2 5.67 us: make_partial(): return jnp.dot(density, factor, preferred_element_type=jnp.float32)]
  transfers between devices with their start and end apart: 6 -> 0, of which waited for: 6 -> 0; matrix products, arithmetic and copies ran while one was open for 2% -> 0% of each run, Pallas kernels for 0% -> 0%
where the time goes in v1:
time: 83.2 us; the launch traced here: 81.5 us
  Pallas kernels  75.6 us (91%)
  local copies, waits for them, and re-layouts  4.63 us (6%)
  between operations  1.32 us (2%)
    pallas_call x1, Pallas kernels, per_device(): pl.pallas_call(kernel, out_shape=jax.ShapeDtypeStruct((512, 512), jnp.flo...  75.6 us
    unnamed x10, local copies, waits for them, and re-layouts  4.63 us

profile of v1, /device:TPU:32, one launch (start us, length us, event | category | flops | bytes accessed | tf_op | source)
XLA Modules:
  0.0 81.5 jit_solution(11994985421699166554)
XLA Ops:
  1.3 0.0 copy-start.3
  1.3 0.6 copy-done.3
  2.0 0.1 copy.7.dm_ref
  2.0 0.0 copy-start
  2.0 1.0 %copy-done = bf16[512,512]{1,0:T(8,128)(2,1)S(1)} copy-done((bf16[512,512]{1,0:T(8,128)(2,1)S(1)}, bf16[512,512]{1,0:T(8,128)(2,1)}, u32[]{:S(2)}) %copy-start) | copy-done | bytes 524312
  3.1 0.0 copy-start.1
  3.1 1.0 %copy-done.1 = bf16[512,512]{1,0:T(8,128)(2,1)S(1)} copy-done((bf16[512,512]{1,0:T(8,128)(2,1)S(1)}, bf16[512,512]{1,0:T(8,128)(2,1)}, u32[]{:S(2)}) %copy-start.1) | copy-done | bytes 524312
  4.1 0.0 copy-start.2
  4.1 0.8 %copy-done.2 = bf16[64,512]{1,0:T(8,128)(2,1)S(1)} copy-done((bf16[64,512]{1,0:T(8,128)(2,1)S(1)}, bf16[64,512]{1,0:T(8,128)(2,1)}, u32[]{:S(2)}) %copy-start.2) | copy-done | bytes 65560
  5.0 75.6 %shard_map.64 = f32[512,512]{1,0:T(8,128)S(1)} custom-call(bf16[512,512]{1,0:T(8,128)(2,1)S(1)} %copy-done, bf16[512,512]{1,0:T(8,128)(2,1)S(1)} %copy-done.1, bf16[4,16,512]{2,1,0:T(8,128)(2,1)S(1)} %bitcast.1, s32[1,1]{1,0:T(1,128)S(6)} %copy.9.fm_ref, s32[1,1]{1,0:T(1,128)S(6)} %copy.10.sm_ref, s32[2,1]{1,0:T(2,128)S(1)} %copy.7.dm_ref), custom_call_target="tpu_custom_call" | custom-call | flops 2147483648 | bytes 3145728 | tf_op jit(solution)/shard_map/pallas_call | solution.py:284
  80.6 1.0 %copy.11 = f32[512,512]{1,0:T(8,128)} copy(f32[512,512]{1,0:T(8,128)S(1)} %shard_map.64) | data formatting | bytes 2097152
Async XLA Ops:
  1.3 0.7 copy-start.3
  2.0 1.0 %copy-start = (bf16[512,512]{1,0:T(8,128)(2,1)S(1)}, bf16[512,512]{1,0:T(8,128)(2,1)}, u32[]{:S(2)}) copy-start(bf16[512,512]{1,0:T(8,128)(2,1)} %f_ref.1) | copy-start | bytes 1572868
  3.1 1.0 %copy-start.1 = (bf16[512,512]{1,0:T(8,128)(2,1)S(1)}, bf16[512,512]{1,0:T(8,128)(2,1)}, u32[]{:S(2)}) copy-start(bf16[512,512]{1,0:T(8,128)(2,1)} %s_ref.1) | copy-start | bytes 1572868
  4.1 0.8 %copy-start.2 = (bf16[64,512]{1,0:T(8,128)(2,1)S(1)}, bf16[64,512]{1,0:T(8,128)(2,1)}, u32[]{:S(2)}) copy-start(bf16[64,512]{1,0:T(8,128)(2,1)} %param.8) | copy-start | bytes 196612

commit v2 on v1

v2 whole, which is shorter than its diff:
```python
import jax
import jax.numpy as jnp
from jax import lax
from jax.experimental import pallas as pl
from jax.experimental.pallas import tpu as pltpu
from jax.sharding import PartitionSpec as P

MESH = pl.DeviceIdType.MESH
NC = 4
LN = 128
SR = 16
HR = 128
HZ = 32
TOP = 32000.0
TINY = 2.0**-100
JOBS = ((0, (0, 1)), (1, (0, 1)), (2, (0, 1)), (3, (0, 1)))
NJ = len(JOBS)
ORDER = (
    "S0", "D.0", "a.0", "a.1", "D.1", "r.0", "r.1", "b.0", "a.2", "b.1", "r.2", "c.0", "a.3", "b.2",
    "r.3", "c.1", "S1", "e.0", "b.3", "c.2", "e.1", "g.0", "S2", "c.3", "e.2", "h.0", "g.1", "e.3",
    "h.1", "g.2", "S3", "h.2", "g.3", "S4", "k.0", "k.1", "h.3", "k.2", "k.3",
)


def encode(value):
    amax = jnp.max(jnp.abs(value), axis=0, keepdims=True)
    t = jnp.ceil(jnp.log2(jnp.maximum(amax, TINY)))
    q = jnp.round(value * (jnp.exp2(-t) * TOP)).astype(jnp.int32).astype(jnp.int16)
    return q, t


def decode(q, t):
    return q.astype(jnp.int32).astype(jnp.float32) * (jnp.exp2(t) * (1.0 / TOP))


def kernel(
    f_hbm, s_hbm, d_hbm, fm_hbm, sm_hbm, dm_hbm, out_ref,
    f_ref, s_ref, d_ref, fm_ref, sm_ref, dm_ref, in_sem,
    w, dg, ys, yr, pf, zs, zr, yq, qg, strips, rn,
    d_ss, d_rs, c_ss, c_rs, t_ss, t_rs, t0_ss, t0_rs,
    ys_ss, ys_rs, zs_ss, zs_rs, za_ss, za_rs, ya_ss, ya_rs,
):
    row, col = lax.axis_index("row"), lax.axis_index("col")
    y, zh = row // 4, row % 4
    zl, x, core = col // 8, (col // 2) % 4, col % 2
    p = zl * 4 + x

    def group_peer(o):
        return (row, ((zl + o // 4) % 2) * 8 + ((x + o % 4) % 4) * 2 + core)

    def chip_of(o):
        return ((zl + o // 4) % 2) * 4 + (x + o % 4) % 4

    def y_peer(d):
        return (((y + d) % 4) * 4 + zh, col)

    def z_peer(d):
        return (y * 4 + (zh + d) % 4, col)

    core_peer = (row, zl * 8 + x * 2 + 1 - core)
    up, down = y_peer(1), y_peer(3)

    started = []

    def copy(src, dst, ss, rs, to):
        return pltpu.make_async_remote_copy(
            src_ref=src, dst_ref=dst, send_sem=ss, recv_sem=rs, device_id=to, device_id_type=MESH
        )

    def send(src, dst, ss, rs, to):
        c = copy(src, dst, ss, rs, to)
        c.start()
        started.append(c)
        return c

    barrier = pltpu.get_barrier_semaphore()
    partners = [z_peer(d) for d in (2, 1, 3)] + [group_peer(o) for o in range(1, 8)]
    partners += [core_peer, up, down]
    for to in partners:
        pl.semaphore_signal(barrier, inc=1, device_id=to, device_id_type=MESH)

    ins = [
        pltpu.make_async_copy(src, dst, in_sem.at[i])
        for i, (src, dst) in enumerate(
            ((d_hbm, d_ref), (dm_hbm, dm_ref), (fm_hbm, fm_ref), (sm_hbm, sm_ref), (f_hbm, f_ref), (s_hbm, s_ref))
        )
    ]
    for cp in ins:
        cp.start()
    for cp in ins[:2]:
        cp.wait()
    dmask = dm_ref[0, zl].astype(jnp.float32)
    for d in range(4):
        rows = d_ref[(y + 2 + d) % 4]
        dg[d, p, core] = (rows.astype(jnp.float32) * dmask).astype(jnp.bfloat16)
    for cp in ins[2:]:
        cp.wait()
    fmask = fm_ref[0, 0].astype(jnp.float32)
    smask = sm_ref[0, 0].astype(jnp.float32)
    pl.semaphore_wait(barrier, len(partners))

    head, tail = pl.ds(0, 1), pl.ds(1, 3)
    d_sent = [
        [
            send(dg.at[part, p, core], dg.at[part, p, core], d_ss.at[i, o], d_rs.at[i, o], group_peer(o))
            for o in range(1, 8)
        ]
        for i, part in enumerate((head, tail))
    ]

    s_all = (s_ref[...].astype(jnp.float32) * smask).astype(jnp.bfloat16)
    f_all = (f_ref[...].astype(jnp.float32) * fmask).astype(jnp.bfloat16)
    for n in range(NC):
        w[n, :, :LN] = s_all[:, n * LN : (n + 1) * LN]
        w[n, :, LN:] = f_all[:, n * LN : (n + 1) * LN]

    @pl.when(p == 0)
    def _():
        for i in range(4):
            strips[core, i] = f_all[i * 128 : (i + 1) * 128]
            strips[core, 4 + i] = s_all[i * 128 : (i + 1) * 128]

    def swap_density(i):
        part = (head, tail)[i]
        for cp in d_sent[i]:
            cp.wait_recv()
        cp = send(dg.at[part, :, core], dg.at[part, :, core], c_ss.at[i], c_rs.at[i], core_peer)
        cp.wait_recv()

    def strip(i):
        return strips.at[core, i]

    def strips_0(_):
        @pl.when(p == 0)
        def _():
            for i in range(1, 8):
                copy(strip(i), strip(i), t0_ss.at[i], t0_rs, (row, 2 * i + core)).start()

    def strips_1(_):
        @pl.when(p != 0)
        def _():
            copy(strip(p), strip(p), t0_ss.at[0], t0_rs, core_peer).wait_recv()

        for o in (4, 2, 1, 3):
            @pl.when(chip_of(o) != 0)
            def _():
                copy(strip(p), strip(p), t_ss.at[o], t_rs.at[o], group_peer(o)).start()

    other = (1 - zl) * 4 + x

    def strips_2(_):
        @pl.when(p != 0)
        def _():
            copy(strip(other), strip(other), t_ss.at[4], t_rs.at[4], core_peer).wait_recv()

        for o in (2, 1, 3):
            @pl.when(chip_of(o) != 0)
            def _():
                copy(strip(other), strip(other), t_ss.at[4 + o], t_rs.at[4 + o], group_peer(o)).start()

    swaps = []

    def strips_3(_):
        @pl.when(p != 0)
        def _():
            for o in (1, 2, 3, 5, 6, 7):
                copy(strip(p), strip(p), t_ss.at[o], t_rs.at[o], core_peer).wait_recv()

        swaps.append(send(strips.at[core], strips.at[core], c_ss.at[2], c_rs.at[2], core_peer))

    def strips_4(_):
        swaps[0].wait_recv()

    def product(d, j):
        n, hs = JOBS[j]
        rows = dg[d, 4 * hs[0] : 4 * hs[-1] + 4].reshape(HR * len(hs), 512)
        return jnp.dot(rows, w[n], preferred_element_type=jnp.float32)

    y_sent = {}

    def send_y(j, i, value):
        q, t = encode(value)
        m = value.shape[0]
        ys[j, i, :m] = q
        ys[j, i, m : m + SR] = jnp.broadcast_to(t, (SR, LN)).astype(jnp.int32).astype(jnp.int16)
        part = pl.ds(0, m + SR)
        y_sent[j, i] = send(
            ys.at[j, i, part], yr.at[j, i, part], ys_ss.at[j, i], ys_rs.at[j, i], down if i % 2 else up
        )

    def recv_y(j, i):
        m = HR * len(JOBS[j][1])
        y_sent[j, i].wait_recv()
        t = yr[j, i, m : m + SR].astype(jnp.int32).astype(jnp.float32)[:1]
        return decode(yr[j, i, :m], t)

    def a(j):
        v = product(0, j)
        send_y(j, 0, v[:, :LN])
        send_y(j, 1, v[:, LN:])

    def r(j):
        m = HR * len(JOBS[j][1])
        v = product(3, j)
        send_y(j, 2, v[:, LN:])
        pf[j, 0, :m] = v[:, :LN]
        v = product(1, j)
        send_y(j, 3, v[:, :LN])
        pf[j, 1, :m] = v[:, LN:]

    def b(j):
        m = HR * len(JOBS[j][1])
        send_y(j, 4, pf[j, 0, :m] + recv_y(j, 0))
        send_y(j, 5, pf[j, 1, :m] + recv_y(j, 1))

    z_sent = {}

    def c(j):
        nh = len(JOBS[j][1])
        v = product(2, j)
        left = v[:, LN:] + recv_y(j, 2)
        right = v[:, :LN] + recv_y(j, 3)
        right = right + recv_y(j, 4)
        left = left + recv_y(j, 5)
        yq[j, 0, :nh] = right.reshape(nh, 4, HZ, LN)
        yq[j, 1, :nh] = left.reshape(nh, 4, HZ, LN)
        m = HZ * nh
        part = pl.ds(0, 2 * m + SR)
        for d in (2, 1, 3):
            to = (zh + d) % 4
            q0, t0 = encode(yq[j, 0, :nh, to].reshape(m, LN))
            q1, t1 = encode(yq[j, 1, :nh, to].reshape(m, LN))
            zs[j, d, :m] = q0
            zs[j, d, m : 2 * m] = q1
            t = jnp.concatenate([jnp.broadcast_to(t0, (8, LN)), jnp.broadcast_to(t1, (8, LN))], axis=0)
            zs[j, d, 2 * m : 2 * m + SR] = t.astype(jnp.int32).astype(jnp.int16)
            z_sent[j, d] = send(zs.at[j, d, part], zr.at[j, d, part], zs_ss.at[j, d], zs_rs.at[j, d], z_peer(d))

    za_sent = {}

    def e(j):
        n, hs = JOBS[j]
        nh = len(hs)
        m = HZ * nh
        right = yq[j, 0, :nh, zh].reshape(m, LN)
        left = yq[j, 1, :nh, zh].reshape(m, LN)
        for d in (1, 3, 2):
            z_sent[j, d].wait_recv()
            t = zr[j, d, 2 * m : 2 * m + SR].astype(jnp.int32).astype(jnp.float32)
            right = right + decode(zr[j, d, :m], t[:1])
            left = left + decode(zr[j, d, m : 2 * m], t[8:9])
        rows = slice(hs[0], hs[0] + nh)
        qg[n, y, 0, rows, zh] = right.astype(jnp.bfloat16).reshape(nh, HZ, LN)
        qg[n, y, 1, rows, zh] = left.astype(jnp.bfloat16).reshape(nh, HZ, LN)
        mine = qg.at[n, y, :, pl.ds(hs[0], nh), zh]
        for d in (2, 1, 3):
            za_sent[j, d] = send(mine, mine, za_ss.at[j, d], za_rs.at[j, d], z_peer(d))

    ya_sent = {}

    def g(j):
        n, hs = JOBS[j]
        for d in (1, 3, 2):
            za_sent[j, d].wait_recv()
        rows = pl.ds(hs[0], len(hs))
        for i, (m, to) in enumerate(((0, up), (1, down), (1, up), (0, down))):
            mine = qg.at[n, y, m, rows]
            ya_sent[j, i] = send(mine, mine, ya_ss.at[j, i], ya_rs.at[j, i], to)

    def h(j):
        n, hs = JOBS[j]
        rows = pl.ds(hs[0], len(hs))
        ya_sent[j, 0].wait_recv()
        part = qg.at[n, (y + 3) % 4, 0, rows]
        ya_sent[j, 4] = send(part, part, ya_ss.at[j, 4], ya_rs.at[j, 4], up)
        ya_sent[j, 1].wait_recv()
        part = qg.at[n, (y + 1) % 4, 1, rows]
        ya_sent[j, 5] = send(part, part, ya_ss.at[j, 5], ya_rs.at[j, 5], down)

    def k(j):
        n, hs = JOBS[j]
        for i in (2, 3, 4, 5):
            ya_sent[j, i].wait_recv()
        at = slice(n * LN, (n + 1) * LN)
        total = None
        for half in hs:
            for m in range(2):
                for q in range(4):
                    for cc in range(8):
                        to = cc * 64 + q * 16
                        rn[m, to : to + 16] = qg[n, q, m, half, cc // 2, (cc % 2) * 16 : (cc % 2) * 16 + 16]
            for m in range(2):
                lhs = strips[half, 4 * m : 4 * m + 4].reshape(512, 512)
                part = jnp.dot(lhs, rn[m], preferred_element_type=jnp.float32)
                total = part if total is None else (total + part if m == 0 else total - part)
        out_ref[:, at] = total if hs[0] == 0 else out_ref[:, at] + total

    steps = {"D": swap_density, "S0": strips_0, "S1": strips_1, "S2": strips_2, "S3": strips_3, "S4": strips_4}
    steps.update(a=a, r=r, b=b, c=c, e=e, g=g, h=h, k=k)
    for word in ORDER:
        name, _, j = word.partition(".")
        steps[name](int(j or 0))

    for cp in started:
        cp.wait_send()

    @pl.when(p == 0)
    def _():
        for i in range(1, 8):
            copy(strip(i), strip(i), t0_ss.at[i], t0_rs, core_peer).wait_send()

    for o in range(1, 8):
        @pl.when(chip_of(o % 4 if o != 4 else 4) != 0)
        def _():
            copy(strip(p), strip(p), t_ss.at[o], t_rs.at[o], core_peer).wait_send()


def per_device(fock_matrix, intersection, density_panel, fock_mask, intersection_mask, density_mask):
    vmem = pl.BlockSpec(memory_space=pltpu.VMEM)
    hbm = pl.BlockSpec(memory_space=pltpu.HBM)
    dma = pltpu.SemaphoreType.DMA
    bf16, f32, i16 = jnp.bfloat16, jnp.float32, jnp.int16
    return pl.pallas_call(
        kernel,
        out_shape=jax.ShapeDtypeStruct((512, 512), jnp.float32),
        in_specs=[hbm] * 6,
        out_specs=vmem,
        scratch_shapes=[
            pltpu.VMEM((512, 512), bf16),
            pltpu.VMEM((512, 512), bf16),
            pltpu.VMEM((4, 16, 512), bf16),
            pltpu.SMEM((1, 1), jnp.int32),
            pltpu.SMEM((1, 1), jnp.int32),
            pltpu.SMEM((1, 2), jnp.int32),
            dma((6,)),
            pltpu.VMEM((NC, 512, 2 * LN), bf16),
            pltpu.VMEM((4, 8, 2, 16, 512), bf16),
            pltpu.VMEM((NJ, 6, 2 * HR + SR, LN), i16),
            pltpu.VMEM((NJ, 6, 2 * HR + SR, LN), i16),
            pltpu.VMEM((NJ, 2, 2 * HR, LN), f32),
            pltpu.VMEM((NJ, 4, 4 * HZ + SR, LN), i16),
            pltpu.VMEM((NJ, 4, 4 * HZ + SR, LN), i16),
            pltpu.VMEM((NJ, 2, 2, 4, HZ, LN), f32),
            pltpu.VMEM((NC, 4, 2, 2, 4, HZ, LN), bf16),
            pltpu.VMEM((2, 8, 128, 512), bf16),
            pltpu.VMEM((2, 512, LN), bf16),
            dma((2, 8)), dma((2, 8)), dma((3,)), dma((3,)), dma((8,)), dma((8,)), dma((8,)), dma(()),
            dma((NJ, 6)), dma((NJ, 6)), dma((NJ, 4)), dma((NJ, 4)), dma((NJ, 4)), dma((NJ, 4)),
            dma((NJ, 6)), dma((NJ, 6)),
        ],
        compiler_params=pltpu.CompilerParams(
            collective_id=0, has_side_effects=True, vmem_limit_bytes=56 * 2**20
        ),
        cost_estimate=pl.CostEstimate(flops=2 * 2**30, bytes_accessed=3 * 2**20, transcendentals=0),
    )(
        fock_matrix,
        intersection,
        density_panel.reshape(4, 16, 512),
        fock_mask,
        intersection_mask,
        density_mask.T,
    )


def solution(mesh):
    placed = (
        P("row", "col"),
        P("row", "col"),
        P("col", "row"),
        P("row", "col"),
        P("row", "col"),
        P(None, "row"),
    )
    return jax.shard_map(
        per_device, mesh=mesh, in_specs=placed, out_specs=P("row", "col"), check_vma=False
    )
```

time: 83.2 us -> 73.1 us (0.88); the launches traced: 81.5 us -> 73 us
  Pallas kernels: 75.6 us -> 69.4 us
  local copies, waits for them, and re-layouts: 4.63 us -> 2.26 us
    pallas_call x1, Pallas kernels: 75.6 us -> 69.4 us  [per_device(): pl.pallas_call(kernel, out_shape=jax.ShapeDtypeStruct((512, 512), jnp.flo...]
    unnamed x10 -> x1, local copies, waits for them, and re-layouts: 4.63 us -> 2.26 us
where the time goes in v2:
time: 73.1 us; the launch traced here: 73 us
  Pallas kernels  69.4 us (95%)
  local copies, waits for them, and re-layouts  2.26 us (3%)
  between operations  1.3 us (2%)
    pallas_call x1, Pallas kernels, per_device(): pl.pallas_call(kernel, out_shape=jax.ShapeDtypeStruct((512, 512), jnp.flo...  69.4 us
    unnamed x1, local copies, waits for them, and re-layouts  2.26 us

profile of v2, /device:TPU:32, one launch (start us, length us, event | category | flops | bytes accessed | tf_op | source)
XLA Modules:
  0.0 73.0 jit_solution(4578074615350404456)
XLA Ops:
  1.3 69.4 %shard_map.64 = f32[512,512]{1,0:T(8,128)} custom-call(bf16[512,512]{1,0:T(8,128)(2,1)} %f_hbm.1, bf16[512,512]{1,0:T(8,128)(2,1)} %s_hbm.1, bf16[4,16,512]{2,1,0:T(8,128)(2,1)} %bitcast.2, s32[1,1]{1,0:T(1,128)S(6)} %copy.8.fm_hbm, s32[1,1]{1,0:T(1,128)S(6)} %copy.9.sm_hbm, s32[1,2]{1,0:T(1,128)} %bitcast.3), custom_call_target="tpu_custom_call" | custom-call | flops 2147483648 | bytes 3145728 | tf_op jit(solution)/shard_map/pallas_call | solution.py:323
  70.7 2.3 %copy.10 = f32[512,512]{1,0:T(8,128)} copy(f32[512,512]{1,0:T(8,128)} %shard_map.64) | data formatting | bytes 2097152

commit v3 on v2

--- a/solution.py
+++ b/solution.py
@@ -17,7 +17,7 @@
 NJ = len(JOBS)
 ORDER = (
     "S0", "D.0", "a.0", "a.1", "D.1", "r.0", "r.1", "b.0", "a.2", "b.1", "r.2", "c.0", "a.3", "b.2",
-    "r.3", "c.1", "S1", "e.0", "b.3", "c.2", "e.1", "g.0", "S2", "c.3", "e.2", "h.0", "g.1", "e.3",
+    "r.3", "c.1", "b.3", "e.0", "S1", "c.2", "e.1", "c.3", "g.0", "S2", "e.2", "h.0", "g.1", "e.3",
     "h.1", "g.2", "S3", "h.2", "g.3", "S4", "k.0", "k.1", "h.3", "k.2", "k.3",
 )
 
@@ -35,7 +35,7 @@
 
 def kernel(
     f_hbm, s_hbm, d_hbm, fm_hbm, sm_hbm, dm_hbm, out_ref,
-    f_ref, s_ref, d_ref, fm_ref, sm_ref, dm_ref, in_sem,
+    f_ref, s_ref, d_ref, fm_ref, sm_ref, dm_ref, in_sem, staged, out_sem,
     w, dg, ys, yr, pf, zs, zr, yq, qg, strips, rn,
     d_ss, d_rs, c_ss, c_rs, t_ss, t_rs, t0_ss, t0_rs,
     ys_ss, ys_rs, zs_ss, zs_rs, za_ss, za_rs, ya_ss, ya_rs,
@@ -93,10 +93,6 @@
     for d in range(4):
         rows = d_ref[(y + 2 + d) % 4]
         dg[d, p, core] = (rows.astype(jnp.float32) * dmask).astype(jnp.bfloat16)
-    for cp in ins[2:]:
-        cp.wait()
-    fmask = fm_ref[0, 0].astype(jnp.float32)
-    smask = sm_ref[0, 0].astype(jnp.float32)
     pl.semaphore_wait(barrier, len(partners))
 
     head, tail = pl.ds(0, 1), pl.ds(1, 3)
@@ -108,6 +104,10 @@
         for i, part in enumerate((head, tail))
     ]
 
+    for cp in ins[2:]:
+        cp.wait()
+    fmask = fm_ref[0, 0].astype(jnp.float32)
+    smask = sm_ref[0, 0].astype(jnp.float32)
     s_all = (s_ref[...].astype(jnp.float32) * smask).astype(jnp.bfloat16)
     f_all = (f_ref[...].astype(jnp.float32) * fmask).astype(jnp.bfloat16)
     for n in range(NC):
@@ -159,6 +159,7 @@
                 copy(strip(other), strip(other), t_ss.at[4 + o], t_rs.at[4 + o], group_peer(o)).start()
 
     swaps = []
+    outs = []
 
     def strips_3(_):
         @pl.when(p != 0)
@@ -281,7 +282,6 @@
         n, hs = JOBS[j]
         for i in (2, 3, 4, 5):
             ya_sent[j, i].wait_recv()
-        at = slice(n * LN, (n + 1) * LN)
         total = None
         for half in hs:
             for m in range(2):
@@ -293,7 +293,11 @@
                 lhs = strips[half, 4 * m : 4 * m + 4].reshape(512, 512)
                 part = jnp.dot(lhs, rn[m], preferred_element_type=jnp.float32)
                 total = part if total is None else (total + part if m == 0 else total - part)
-        out_ref[:, at] = total if hs[0] == 0 else out_ref[:, at] + total
+        staged[n] = total if hs[0] == 0 else staged[n] + total
+        if hs[-1] == 1:
+            out = pltpu.make_async_copy(staged.at[n], out_ref.at[:, pl.ds(n * LN, LN)], out_sem.at[n])
+            out.start()
+            outs.append(out)
 
     steps = {"D": swap_density, "S0": strips_0, "S1": strips_1, "S2": strips_2, "S3": strips_3, "S4": strips_4}
     steps.update(a=a, r=r, b=b, c=c, e=e, g=g, h=h, k=k)
@@ -301,6 +305,8 @@
         name, _, j = word.partition(".")
         steps[name](int(j or 0))
 
+    for cp in outs:
+        cp.wait()
     for cp in started:
         cp.wait_send()
 
@@ -316,7 +322,6 @@
 
 
 def per_device(fock_matrix, intersection, density_panel, fock_mask, intersection_mask, density_mask):
-    vmem = pl.BlockSpec(memory_space=pltpu.VMEM)
     hbm = pl.BlockSpec(memory_space=pltpu.HBM)
     dma = pltpu.SemaphoreType.DMA
     bf16, f32, i16 = jnp.bfloat16, jnp.float32, jnp.int16
@@ -324,7 +329,7 @@
         kernel,
         out_shape=jax.ShapeDtypeStruct((512, 512), jnp.float32),
         in_specs=[hbm] * 6,
-        out_specs=vmem,
+        out_specs=pl.BlockSpec(memory_space=pl.ANY),
         scratch_shapes=[
             pltpu.VMEM((512, 512), bf16),
             pltpu.VMEM((512, 512), bf16),
@@ -333,6 +338,8 @@
             pltpu.SMEM((1, 1), jnp.int32),
             pltpu.SMEM((1, 2), jnp.int32),
             dma((6,)),
+            pltpu.VMEM((NC, 512, LN), f32),
+            dma((NC,)),
             pltpu.VMEM((NC, 512, 2 * LN), bf16),
             pltpu.VMEM((4, 8, 2, 16, 512), bf16),
             pltpu.VMEM((NJ, 6, 2 * HR + SR, LN), i16),

time: 73.1 us -> 72.7 us (level)
  Pallas kernels: 69.4 us -> 68.3 us
    pallas_call x1, Pallas kernels: 69.4 us -> 68.3 us  [per_device(): pl.pallas_call(kernel, out_shape=jax.ShapeDtypeStruct((512, 512), jnp.flo...]
where the time goes in v3:
time: 72.7 us; the launch traced here: 71.9 us
  Pallas kernels  68.3 us (94%)
  local copies, waits for them, and re-layouts  2.26 us (3%)
  between operations  1.3 us (2%)
    pallas_call x1, Pallas kernels, per_device(): pl.pallas_call(kernel, out_shape=jax.ShapeDtypeStruct((512, 512), jnp.flo...  68.3 us
    unnamed x1, local copies, waits for them, and re-layouts  2.26 us

profile of v3, /device:TPU:32, one launch (start us, length us, event | category | flops | bytes accessed | tf_op | source)
XLA Modules:
  0.0 71.9 jit_solution(7196551186293192466)
XLA Ops:
  1.3 68.3 %shard_map.64 = f32[512,512]{1,0:T(8,128)} custom-call(bf16[512,512]{1,0:T(8,128)(2,1)} %f_hbm.1, bf16[512,512]{1,0:T(8,128)(2,1)} %s_hbm.1, bf16[4,16,512]{2,1,0:T(8,128)(2,1)} %bitcast.2, s32[1,1]{1,0:T(1,128)S(6)} %copy.8.fm_hbm, s32[1,1]{1,0:T(1,128)S(6)} %copy.9.sm_hbm, s32[1,2]{1,0:T(1,128)} %bitcast.3), custom_call_target="tpu_custom_call" | custom-call | flops 2147483648 | bytes 3145728 | tf_op jit(solution)/shard_map/pallas_call | solution.py:328
  69.6 2.3 %copy.10 = f32[512,512]{1,0:T(8,128)} copy(f32[512,512]{1,0:T(8,128)} %shard_map.64) | data formatting | bytes 2097152

commit v4 on v3

--- a/solution.py
+++ b/solution.py
@@ -13,12 +13,13 @@
 HZ = 32
 TOP = 32000.0
 TINY = 2.0**-100
-JOBS = ((0, (0, 1)), (1, (0, 1)), (2, (0, 1)), (3, (0, 1)))
+JOBS = ((0, (0, 1)), (1, (0, 1)), (2, (0, 1)), (3, (0,)), (3, (1,)))
 NJ = len(JOBS)
 ORDER = (
-    "S0", "D.0", "a.0", "a.1", "D.1", "r.0", "r.1", "b.0", "a.2", "b.1", "r.2", "c.0", "a.3", "b.2",
-    "r.3", "c.1", "b.3", "e.0", "S1", "c.2", "e.1", "c.3", "g.0", "S2", "e.2", "h.0", "g.1", "e.3",
-    "h.1", "g.2", "S3", "h.2", "g.3", "S4", "k.0", "k.1", "h.3", "k.2", "k.3",
+    "S0", "D.0", "a.0", "a.1", "D.1", "r.0", "r.1", "b.0", "a.2", "b.1", "r.2", "c.0", "a.3", "a.4",
+    "b.2", "r.3", "r.4", "c.1", "b.3", "e.0", "b.4", "S1", "c.2", "e.1", "c.3", "g.0", "S2", "c.4",
+    "e.2", "h.0", "g.1", "e.3", "e.4", "h.1", "g.2", "S3", "h.2", "g.3", "g.4", "S4", "k.0", "k.1",
+    "h.3", "h.4", "k.2", "k.3", "k.4",
 )
 
 

time: 72.7 us -> 74.3 us (1.022)
  Pallas kernels: 68.3 us -> 70.6 us
    pallas_call x1, Pallas kernels: 68.3 us -> 70.6 us  [per_device(): pl.pallas_call(kernel, out_shape=jax.ShapeDtypeStruct((512, 512), jnp.flo...]
where the time goes in v4:
time: 74.3 us; the launch traced here: 74.1 us
  Pallas kernels  70.6 us (95%)
  local copies, waits for them, and re-layouts  2.26 us (3%)
  between operations  1.3 us (2%)
    pallas_call x1, Pallas kernels, per_device(): pl.pallas_call(kernel, out_shape=jax.ShapeDtypeStruct((512, 512), jnp.flo...  70.6 us
    unnamed x1, local copies, waits for them, and re-layouts  2.26 us

profile of v4, /device:TPU:32, one launch (start us, length us, event | category | flops | bytes accessed | tf_op | source)
XLA Modules:
  0.0 74.1 jit_solution(9490114016370365444)
XLA Ops:
  1.3 70.6 %shard_map.64 = f32[512,512]{1,0:T(8,128)} custom-call(bf16[512,512]{1,0:T(8,128)(2,1)} %f_hbm.1, bf16[512,512]{1,0:T(8,128)(2,1)} %s_hbm.1, bf16[4,16,512]{2,1,0:T(8,128)(2,1)} %bitcast.2, s32[1,1]{1,0:T(1,128)S(6)} %copy.8.fm_hbm, s32[1,1]{1,0:T(1,128)S(6)} %copy.9.sm_hbm, s32[1,2]{1,0:T(1,128)} %bitcast.3), custom_call_target="tpu_custom_call" | custom-call | flops 2147483648 | bytes 3145728 | tf_op jit(solution)/shard_map/pallas_call | solution.py:329
  71.9 2.3 %copy.10 = f32[512,512]{1,0:T(8,128)} copy(f32[512,512]{1,0:T(8,128)} %shard_map.64) | data formatting | bytes 2097152
